TPU v7x, 128 devices: a whole 4x4x4 slice. The times are simulated.
128 devices in a mesh: lon: 16 (over z_lo, x, core), lat: 8 (over z_hi, y).
Axes of the slice: x: 4, y: 4, z: 4 (z_hi: 2, z_lo: 2; z = z_hi * 2 + z_lo), core: 2. Of those that a mesh axis runs over, the one named last changes fastest.
Arguments:
- tracers: float32 [8, 1440, 72, 128], P('lat', 'lon'), may hold values from -6 to 6
- offsets: int32 [8], P('lat'), may hold values from -180 to 180, as said below
- fraction: float32 [8], P('lat'), may hold values from 0 to 1
- cutoffs: int32 [8], P('lat'), may hold values from 1 to 48, as said below
- keep_high: float32 [8], P('lat'), may hold values from 0.1 to 0.5
- mixing: float32 [8], P('lat'), may hold values from 0.05 to 0.24
- kz: float32 [8, 1440, 72], P('lat', 'lon'), may hold values from 0.05 to 20
- light: float32 [8, 1440], P('lat', 'lon'), may hold values from 0.2 to 1.5
- loss_rate: float32 [72, 128], replicated, may hold values from 0.02 to 4
- source: float32 [72, 128], replicated, may hold values from -3 to 3
Outputs:
- updated: float32 [8, 1440, 72, 128], P('lat', 'lon')
Inputs may be any that keep to these rules, and one draw needn't show every extreme that they name: `offsets`: row r's offset has magnitude at most 180 * min(r + 2, 8) // 8; row 7 has offset 180 and row 6 has offset -180. `cutoffs`: row 0 keeps 48 wavenumbers and row 7 keeps 1.
All inputs are finite; a program needn't handle non-finite values.
Results may differ from a plain program's by a relative error of at most 0.0003.
Values sent between devices are 32-bit elements; how exact they have to be, the bound alone decides.
A program may use at most 64 MiB of HBM per device.

v0:
```python
import math

import jax
import jax.numpy as jnp
from jax import lax
from jax.sharding import PartitionSpec as P

KMAX = 48
REACH = 2


def passed_along(array, axis, by):
    count = lax.axis_size(axis)
    return lax.ppermute(array, axis, [(i, (i + by) % count) for i in range(count)])


def extended_2(array, sides, width):
    for axis, dim in sides:
        count, length = (lax.axis_size(axis), array.shape[dim])
        up = [(i, (i + 1) % count) for i in range(count - 1)]
        down = [(j, i) for i, j in up]
        last = lax.slice_in_dim(array, length - width, length, axis=dim)
        first = lax.slice_in_dim(array, 0, width, axis=dim)
        before = lax.ppermute(last, axis, up)
        after = lax.ppermute(first, axis, down)
        array = jnp.concatenate([before, array, after], axis=dim)
    return array


def column_solve(field, coupling):
    nothing = jnp.zeros_like(coupling[..., :1])
    above = jnp.concatenate([coupling[..., 1:], nothing], axis=-1)
    below = jnp.concatenate([nothing, -coupling[..., 1:]], axis=-1)
    return lax.linalg.tridiagonal_solve(below, 1.0 + coupling + above, -above, field)


def slide_rows(upper_block, lower_block, offsets, fraction):
    width = upper_block.shape[1]
    quotient = jnp.floor_divide(offsets, width)
    remain = offsets - quotient * width
    joined = jnp.concatenate([lower_block, upper_block], axis=1)

    def window_of(one_row, begin):
        return lax.dynamic_slice_in_dim(one_row, begin, width + 1, axis=0)

    window = jax.vmap(window_of)(joined, width - remain - 1)
    weight = fraction[:, None, None]
    return (1.0 - weight) * window[:, 1:] + weight * window[:, :-1]


def wave_table(first, count, total):
    places = first + lax.iota(jnp.int32, count)
    waves = lax.iota(jnp.int32, KMAX + 1)
    phase = (places[:, None] * waves[None, :] % total).astype(jnp.float32) * (2.0 * math.pi / total)
    return jnp.concatenate([jnp.cos(phase), jnp.sin(phase)], axis=1)


def wave_weights(cutoffs, total):
    waves = lax.iota(jnp.int32, KMAX + 1)
    base_weight = jnp.where(waves == 0, 1.0, 2.0) / total
    single = jnp.where(waves[None, :] <= cutoffs[:, None], base_weight[None, :], 0.0)
    return jnp.concatenate([single, single], axis=1)


def project(table, moved):
    return jnp.einsum("ik,rif->rkf", table, moved, precision=lax.Precision.HIGHEST)


def rebuild(table, spectra, weights):
    return jnp.einsum(
        "ik,rkf->rif", table, spectra * weights[:, :, None], precision=lax.Precision.HIGHEST
    )


def chosen(flags):
    return flags[:, None, None]


def body(tracers, offsets, fraction, cutoffs, keep_high, mixing, kz, light, loss_rate, source):
    row_count, width, levels, species = tracers.shape
    depth = levels * species
    cycle_count = lax.axis_size("lon")
    total = width * cycle_count
    settled = column_solve(tracers, kz).reshape(row_count, width, depth)
    weights = wave_weights(cutoffs, total)
    keep_factor = keep_high[:, None, None]
    quotient = jnp.floor_divide(offsets, width)
    upper_block = settled
    lower_block = settled
    eastern = settled
    for distance in range(1, REACH + 2):
        eastern = passed_along(eastern, "lon", 1)
        upper_block = jnp.where(chosen(quotient == distance), eastern, upper_block)
        lower_block = jnp.where(chosen(quotient + 1 == distance), eastern, lower_block)
    western = settled
    for distance in range(1, REACH + 1):
        western = passed_along(western, "lon", -1)
        upper_block = jnp.where(chosen(-quotient == distance), western, upper_block)
        lower_block = jnp.where(chosen(-quotient - 1 == distance), western, lower_block)
    moved = slide_rows(upper_block, lower_block, offsets, fraction)
    table = wave_table(lax.axis_index("lon") * width, width, total)
    spectra = lax.psum(project(table, moved), "lon")
    lowpass = rebuild(table, spectra, weights)
    filtered = keep_factor * moved + (1.0 - keep_factor) * lowpass
    padded = extended_2(filtered, (("lat", 0),), 1)
    band_index = lax.axis_index("lat")
    southern = jnp.where(band_index == 0, filtered, padded[:1])
    northern = jnp.where(band_index == lax.axis_size("lat") - 1, filtered, padded[-1:])
    extended = jnp.concatenate([southern, padded[1:-1], northern], axis=0)
    spread = filtered + mixing[:, None, None] * (extended[:-2] + extended[2:] - 2.0 * filtered)
    spread = spread.reshape(row_count, width, levels, species)
    glow = light[:, :, None, None]
    return (spread + source * glow) / (1.0 + loss_rate * glow)


def solution(mesh):
    return jax.shard_map(
        body,
        mesh=mesh,
        in_specs=(
            P("lat", "lon", None, None),
            P("lat"),
            P("lat"),
            P("lat"),
            P("lat"),
            P("lat"),
            P("lat", "lon", None),
            P("lat", "lon"),
            P(),
            P(),
        ),
        out_specs=P("lat", "lon", None, None),
        check_vma=False,
    )
```

profile of v0, /device:TPU:87, one launch (start us, length us, event | category | flops | bytes accessed | tf_op | source)
XLA Modules:
  0.0 490.1 jit_solution(1004730487204755577)
XLA Ops:
  9.1 2.3 slice.1378
  16.3 2.1 broadcast.256.clone
  18.4 57.9 %while.33 = (s32[]{:T(128)}, f32[1,90]{1,0:T(1,128)S(1)}, f32[1,90,128]{2,1,0:T(8,128)S(1)}, f32[2,32,1,90]{3,1,2,0:T(8,128)}, f32[2,32,1,90,128]{4,3,1,2,0:T(8,...) while((s32[]{:T(128)}, f32[1,90]{1,0:T(1,128)S(1)}, ...), condition=%wide.region_1.2_spmd, body=%wide.region_0.1_spmd.sunk | while | flops 1667553 | bytes 33454160 | solution.py:34
  77.0 2.1 constant_dynamic-update-slice_fusion.97
  88.5 8.1 %while.34 = (s32[]{:T(128)}, f32[1,90,128]{2,1,0:T(8,128)S(1)}, f32[2,32,1,90,128]{4,3,1,2,0:T(8,128)}, f32[2,32,1,90,128]{4,3,2,1,0:T(8,128)S(1)}, f32[2,32,1,9...) while((s32[]{:T(128)}, f32[1,90,128]{2,1,0:T(8,128)S(1)}, ...), condition=%wide.region_3.4_spmd, body=%wide.region_2.3_spmd.sunk | while | flops 1105953 | bytes 33012468 | solution.py:34
  99.0 3.6 copy.275
  102.7 11.0 %concatenate.45 = f32[71,1,90,128]{3,0,1,2:T(8,128)} concatenate(f32[1,1,90,128]{3,0,1,2:T(1,128)S(1)} %copy.268, f32[1,1,90,128]{3,0,1,2:T(1,128)S(1)} %copy.269, f32[1,1,90,128]{3,0,1,2:T(1,128)S(1)} %copy.270, f32[1,1,90,128]{3,0,1,2:T(1,128)S(1)} %copy.271, f32[1,1,90,128]{3,0,1,2:T(1,128)S(1)} %copy.272, f32[1,1,90,128]{3,0,1,2:T(1,128)S(1)} %copy.273, ...), dimensions={0} | concatenate | bytes 6543360 | tf_op jit(solution)/shard_map/vmap(vmap())/concatenate | solution.py:34
  113.7 2.3 pad_maximum_fusion
  117.9 36.1 %collective-permute-done.2 = f32[1,90,9216]{2,0,1:T(1,128)S(1)} collective-permute-done((f32[1,90,9216]{2,0,1:T(1,128)S(1)}, f32[1,90,9216]{2,0,1:T(1,128)S(1)}, u32[]{:S(2)}, u32[]{:S(2)}) %collective-permute-start.2) | collective-permute-done | bytes 3317792 | tf_op jit(solution)/shard_map/ppermute | solution.py:14
  153.9 4.6 collective-permute-start.3
  158.6 35.9 %collective-permute-done.3 = f32[1,90,9216]{2,0,1:T(1,128)} collective-permute-done((f32[1,90,9216]{2,0,1:T(1,128)S(1)}, f32[1,90,9216]{2,0,1:T(1,128)}, u32[]{:S(2)}, u32[]{:S(2)}) %collective-permute-start.3) | collective-permute-done | bytes 3317792 | tf_op jit(solution)/shard_map/ppermute | solution.py:14
  194.6 4.7 collective-permute-start.4
  201.0 34.7 %collective-permute-done.4 = f32[1,90,9216]{2,0,1:T(1,128)} collective-permute-done((f32[1,90,9216]{2,0,1:T(1,128)}, f32[1,90,9216]{2,0,1:T(1,128)}, u32[]{:S(2)}, u32[]{:S(2)}) %collective-permute-start.4) | collective-permute-done | bytes 3317792 | tf_op jit(solution)/shard_map/ppermute | solution.py:14
  235.7 8.5 %select_select_fusion = (f32[1,90,9216]{2,1,0:T(8,128)S(1)}, f32[1,90,9216]{2,1,0:T(8,128)S(1)}) fusion(f32[1,90,9216]{2,0,1:T(1,128)} %collective-permute-done.1, f32[1,90,9216]{2,0,1:T(1,128)} %collective-permute-done, f32[1,90,9216]{2,0,1:T(1,128)} %collective-permute-done.4, f32[1,90,9216]{2,0,1:T(1,128)} %collective-permute-done.3, ...), kind=kLoop, calls=%fused_computation.630 | loop fusion | flops 8294400 | bytes 26542090 | tf_op jit(solution)/shard_map/jit(_where)/select_n | solution.py:98
  247.6 6.2 %convolution_bitcast_fusion = f32[1,98,9216]{2,1,0:T(8,128)} fusion(f32[1,91,9216]{2,1,0:T(8,128)S(1)} %fusion.292, f32[]{:T(128)} %bitcast.2187, f32[]{:T(128)} %bitcast.416, f32[90,49]{1,0:T(8,128)S(1)} %get-tuple-element.498, f32[90,49]{1,0:T(8,128)S(1)} %get-tuple-element.497), kind=kOutput, calls=%fused_computation.611 | convolution fusion | flops 977918592 | bytes 10788872 | tf_op jit(solution)/shard_map/ik,rif->rkf/dot_general | solution.py:66
  255.1 129.5 %all-reduce.3.cloned.1.call-done = f32[1,98,9216]{2,1,0:T(8,128)} async-done(((f32[1,98,9216]{2,1,0:T(8,128)}), f32[1,98,9216]{2,1,0:T(8,128)}) %all-reduce.3.cloned.1.call-update) | async-done | bytes 3612688 | tf_op jit(solution)/shard_map/psum | solution.py:102
  384.7 8.8 %fusion.289 = f32[1,90,9216]{2,1,0:T(8,128)S(1)} fusion(f32[1,98,9216]{2,1,0:T(8,128)} %all-reduce.3.cloned.1.call-done, f32[98]{0:T(128)S(1)} %maximum_bitcast_fusion, f32[]{:T(128)} %bitcast.540, f32[]{:T(128)} %bitcast.2189, f32[1,91,9216]{2,1,0:T(8,128)} %copy-done, f32[]{:T(128)} %bitcast.2186, f32[]{:T(128)} %bitcast.416, f32[90,49]{1,0:T(8,128)} %copy-done.8, ...), kind=kOutput, calls=%fused_computation.614 | convolution fusion | flops 981310080 | bytes 13601640 | tf_op jit(solution)/shard_map/ik,rkf->rif/dot_general | solution.py:70
  393.5 5.4 %copy.289 = f32[1,90,9216]{2,0,1:T(1,128)} copy(f32[1,90,9216]{2,1,0:T(8,128)S(1)} %fusion.289) | data formatting | bytes 6635520 | tf_op jit(solution)/shard_map/add | solution.py:104
  398.9 2.2 collective-permute-start.6
  401.0 4.8 collective-permute-start.5
  406.5 65.8 %collective-permute-done.6 = f32[1,90,9216]{2,0,1:T(1,128)} collective-permute-done((f32[1,90,9216]{2,0,1:T(1,128)}, f32[1,90,9216]{2,0,1:T(1,128)}, u32[]{:S(2)}, u32[]{:S(2)}) %collective-permute-start.6) | collective-permute-done | bytes 3317792 | tf_op jit(solution)/shard_map/ppermute | solution.py:25
  472.3 3.1 collective-permute-done.5
  475.4 4.6 fusion.298
  480.8 2.5 fusion.300
  (312 shorter events, 91.4 us)
Async XLA Ops:
  6.5 378.2 %all-reduce.3.cloned.1.call-start = ((), (), s32[]{:S(2)}) async-start(), calls=%async_computation | async-start | bytes 7667712 | tf_op jit(solution)/shard_map/psum | solution.py:102
  14.5 1.7 copy-start.3
  41.6 3.5 copy-start.9
  41.7 3.5 copy-start.1
  45.4 1.7 copy-start.2
  70.8 3.5 copy-start.9
  70.9 3.5 copy-start.1
  74.6 1.7 copy-start.2
  77.0 2.1 copy-start.17
  77.0 3.9 copy-start.16
  77.0 5.8 %copy-start.15 = (f32[90]{0:T(128)S(1)}, f32[90]{0:T(128)}, u32[]{:S(2)}) copy-start(f32[90]{0:T(128)} %get-tuple-element.484) | copy-start | bytes 1084
  88.6 2.1 copy-start.4
  92.6 2.1 copy-start.4
  116.0 37.9 %collective-permute-start.2 = (f32[1,90,9216]{2,0,1:T(1,128)S(1)}, f32[1,90,9216]{2,0,1:T(1,128)S(1)}, u32[]{:S(2)}, u32[]{:S(2)}) collective-permute-start(f32[1,90,9216]{2,0,1:T(1,128)S(1)} %bitcast.2207), channel_id=1, source_target_pairs={{0,8},{8,16},{16,24},{24,32},{32,40},{40,48},{48,56},{56,64},{64,7... | collective-permute-start | bytes 9953288 | tf_op jit(solution)/shard_map/ppermute | solution.py:14
  117.9 40.8 %collective-permute-start = (f32[1,90,9216]{2,0,1:T(1,128)S(1)}, f32[1,90,9216]{2,0,1:T(1,128)}, u32[]{:S(2)}, u32[]{:S(2)}) collective-permute-start(f32[1,90,9216]{2,0,1:T(1,128)S(1)} %bitcast.2208), channel_id=1, source_target_pairs={{0,120},{8,0},{16,8},{24,16},{32,24},{40,32},{48,40},{56,48},{64,5... | collective-permute-start | bytes 9953288 | tf_op jit(solution)/shard_map/ppermute | solution.py:14
  153.9 4.7 copy-start.6
  153.9 40.6 %collective-permute-start.3 = (f32[1,90,9216]{2,0,1:T(1,128)S(1)}, f32[1,90,9216]{2,0,1:T(1,128)}, u32[]{:S(2)}, u32[]{:S(2)}) collective-permute-start(f32[1,90,9216]{2,0,1:T(1,128)S(1)} %collective-permute-done.2), channel_id=1, source_target_pairs={{0,8},{8,16},{16,24},{24,32},{32,40},{40,48},{48,56},{56,64},{64,7... | collective-permute-start | bytes 9953288 | tf_op jit(solution)/shard_map/ppermute | solution.py:14
  158.6 42.3 %collective-permute-start.1 = (f32[1,90,9216]{2,0,1:T(1,128)}, f32[1,90,9216]{2,0,1:T(1,128)}, u32[]{:S(2)}, u32[]{:S(2)}) collective-permute-start(f32[1,90,9216]{2,0,1:T(1,128)} %collective-permute-done), channel_id=1, source_target_pairs={{0,120},{8,0},{16,8},{24,16},{32,24},{40,32},{48,40},{56,48},{64,5... | collective-permute-start | bytes 9953288 | tf_op jit(solution)/shard_map/ppermute | solution.py:14
  194.6 41.1 %collective-permute-start.4 = (f32[1,90,9216]{2,0,1:T(1,128)}, f32[1,90,9216]{2,0,1:T(1,128)}, u32[]{:S(2)}, u32[]{:S(2)}) collective-permute-start(f32[1,90,9216]{2,0,1:T(1,128)} %collective-permute-done.3), channel_id=1, source_target_pairs={{0,8},{8,16},{16,24},{24,32},{32,40},{40,48},{48,56},{56,64},{64,7... | collective-permute-start | bytes 9953288 | tf_op jit(solution)/shard_map/ppermute | solution.py:14
  200.9 44.9 %copy-start.7 = (f32[90,49]{1,0:T(8,128)}, f32[90,49]{1,0:T(8,128)S(1)}, u32[]{:S(2)}) copy-start(f32[90,49]{1,0:T(8,128)S(1)} %get-tuple-element.497) | copy-start | bytes 52924
  200.9 44.9 %copy-start.8 = (f32[90,49]{1,0:T(8,128)}, f32[90,49]{1,0:T(8,128)S(1)}, u32[]{:S(2)}) copy-start(f32[90,49]{1,0:T(8,128)S(1)} %get-tuple-element.498) | copy-start | bytes 52924
  245.8 1.8 copy-start
  398.9 73.4 %collective-permute-start.6 = (f32[1,90,9216]{2,0,1:T(1,128)}, f32[1,90,9216]{2,0,1:T(1,128)}, u32[]{:S(2)}, u32[]{:S(2)}) collective-permute-start(f32[1,90,9216]{2,0,1:T(1,128)} %copy.289), channel_id=1, source_target_pairs={{1,0},{2,1},{3,2},{4,3},{5,4},{6,5},{7,6},{9,8},{10,9},{11,10},{12... | collective-permute-start | bytes 9953288 | tf_op jit(solution)/shard_map/ppermute | solution.py:25
  401.0 74.4 %collective-permute-start.5 = (f32[1,90,9216]{2,0,1:T(1,128)}, f32[1,90,9216]{2,0,1:T(1,128)}, u32[]{:S(2)}, u32[]{:S(2)}) collective-permute-start(f32[1,90,9216]{2,0,1:T(1,128)} %copy.289), channel_id=1, source_target_pairs={{0,1},{1,2},{2,3},{3,4},{4,5},{5,6},{6,7},{8,9},{9,10},{10,11},{11... | collective-permute-start | bytes 9953288 | tf_op jit(solution)/shard_map/ppermute | solution.py:24
  (9 other events, 8.4 us)
Sparse Core Ops, SparseCore 0:
  253.9 130.7 all-reduce.2
where the time goes:
time: 499 us; the launch traced here: 490 us
  waiting for transfers between devices  305 us (61%)
  other arithmetic  84.3 us (17%)
  local copies, waits for them, and re-layouts  49.3 us (10%)
  starting transfers between devices  18.1 us (4%)
  between operations  17.1 us (3%)
  matrix products  14.9 us (3%)
    psum x1, waiting for transfers between devices, body(): spectra = lax.psum(project(table, moved), 'lon')  130 us
    ppermute x5, waiting for transfers between devices, passed_along(): lax.ppermute(array, axis, [(i, (i + by) % count) for i in range(count)])  107 us
    ppermute x1, waiting for transfers between devices, extended_2(): after = lax.ppermute(first, axis, down)  65.8 us
    while x152, other arithmetic  51 us
    ppermute x5, starting transfers between devices, passed_along(): lax.ppermute(array, axis, [(i, (i + by) % count) for i in range(count)])  11.2 us
    concatenate x4, local copies, waits for them, and re-layouts, column_solve(): lax.linalg.tridiagonal_solve(below, 1.0 + coupling + above, -above, field)  11 us
  transfers between devices with their start and end apart: 8, of which 7 were waited for; matrix products, arithmetic and copies ran while one was open for 0% of the time, Pallas kernels for 0%

commit v1 on v0

v1 whole, which is shorter than its diff:
```python
import functools
import math

import jax
import jax.numpy as jnp
import numpy as np
from jax import lax
from jax.experimental import pallas as pl
from jax.experimental.pallas import tpu as pltpu
from jax.sharding import PartitionSpec as P

NLON = 1440
KMAX = 48
MESH = pl.DeviceIdType.MESH
CELLS = 90
PEERS = 8
HALF = CELLS * PEERS
TILES = 9
EDGE = 184
KPAD = 56
LEFT = EDGE
RIGHT = EDGE + HALF


def split_bf16(table):
    import ml_dtypes

    high = table.astype(ml_dtypes.bfloat16)
    low = (table - high.astype(np.float64)).astype(ml_dtypes.bfloat16)
    return high, low


def wave_tables():
    places = np.arange(HALF)
    waves = np.arange(KMAX + 1)
    phase = (places[:, None] * waves[None, :] % NLON) * (2.0 * math.pi / NLON)
    table = np.zeros((HALF, 2 * KPAD))
    table[:, : KMAX + 1] = np.cos(phase)
    table[:, KPAD : KPAD + KMAX + 1] = np.sin(phase)
    high, low = split_bf16(table)
    rebuild = np.concatenate([high, low], axis=1)
    project = np.ascontiguousarray(rebuild.T)
    shifts = np.arange(-EDGE, EDGE)
    phase = (shifts[:, None] * waves[None, :] % NLON) * (2.0 * math.pi / NLON)
    turn = np.zeros((2 * EDGE, 128), np.float32)
    turn[:, : KMAX + 1] = np.cos(phase)
    turn[:, KPAD : KPAD + KMAX + 1] = np.sin(phase)
    return project, rebuild, turn


def kernel(
    off_ref,
    frac_ref,
    cut_ref,
    keep_ref,
    mix_ref,
    light_ref,
    tracers_ref,
    kz_ref,
    loss_ref,
    source_ref,
    project_ref,
    rebuild_ref,
    turn_ref,
    out_ref,
    inp,
    kbuf,
    glow,
    rot,
    dp,
    cp,
    got,
    circ,
    edge,
    edge_in,
    spec,
    spec_in,
    rows,
    back,
    outb,
    in_sem,
    fs,
    fr,
    es,
    er,
    ss,
    sr,
    ls,
    lr,
    bs,
    br,
    out_sem,
):
    lon = lax.axis_index("lon")
    lat = lax.axis_index("lat")
    me = lon % PEERS
    base = lon - me
    other = {"lon": (lon + PEERS) % (2 * PEERS), "lat": lat}
    has_south = lat > 0
    has_north = lat < 7

    def peer(p):
        return {"lon": base + p, "lat": lat}

    def tile_in(j):
        return pltpu.make_async_copy(
            tracers_ref.at[:, pl.ds(pl.multiple_of(j * 8, 8), 8), :], inp.at[j], in_sem.at[j]
        )

    def tile_out(j):
        return pltpu.make_async_copy(
            outb.at[j], out_ref.at[:, pl.ds(pl.multiple_of(j * 8, 8), 8), :], out_sem.at[j]
        )

    def forth(j, src, dst, to):
        return pltpu.make_async_remote_copy(
            dp.at[j, src], got.at[j, dst], fs.at[j, src], fr.at[j, dst],
            device_id=peer(to), device_id_type=MESH,
        )

    def home(j, src, dst, to):
        return pltpu.make_async_remote_copy(
            got.at[j, src], back.at[j, dst], bs.at[j, src], br.at[j, dst],
            device_id=peer(to), device_id_type=MESH,
        )

    def edge_copy(j):
        return pltpu.make_async_remote_copy(
            edge.at[j], edge_in.at[j], es.at[j], er.at[j],
            device_id=other, device_id_type=MESH,
        )

    def spec_copy(j):
        return pltpu.make_async_remote_copy(
            spec.at[j], spec_in.at[j], ss.at[j], sr.at[j],
            device_id=other, device_id_type=MESH,
        )

    def row_copy(j, slot, to):
        return pltpu.make_async_remote_copy(
            rows.at[2, j], rows.at[slot, j], ls.at[slot, j], lr.at[slot, j],
            device_id={"lon": lon, "lat": to}, device_id_type=MESH,
        )

    def start_in(j, carry):
        tile_in(j).start()
        return carry

    lax.fori_loop(0, TILES, start_in, 0)

    barrier = pltpu.get_barrier_semaphore()
    for d in range(1, PEERS):
        pl.semaphore_signal(barrier, inc=1, device_id=peer((me + d) % PEERS), device_id_type=MESH)
    pl.semaphore_signal(barrier, inc=1, device_id=other, device_id_type=MESH)

    @pl.when(has_south)
    def _():
        pl.semaphore_signal(
            barrier, inc=1, device_id={"lon": lon, "lat": lat - 1}, device_id_type=MESH
        )

    @pl.when(has_north)
    def _():
        pl.semaphore_signal(
            barrier, inc=1, device_id={"lon": lon, "lat": lat + 1}, device_id_type=MESH
        )

    off = off_ref[0]
    frac = frac_ref[0]
    keep = keep_ref[0]
    mix = mix_ref[0]
    kbuf[...] = jnp.zeros_like(kbuf)
    kbuf[:, 0:72] = kz_ref[...]

    def light_row(c, carry):
        glow[pl.ds(c, 1), :] = jnp.full((1, 128), light_ref[0, c], jnp.float32)
        return carry

    lax.fori_loop(0, CELLS, light_row, 0)

    lane = lax.broadcasted_iota(jnp.int32, (1, 128), 1)
    wave = lane % KPAD
    share = jnp.where(wave <= cut_ref[0], jnp.where(wave == 0, 1.0, 2.0) / NLON, 0.0) * (1.0 - keep)
    turn = (1.0 - frac) * turn_ref[pl.ds(EDGE + off, 1), :] + frac * turn_ref[pl.ds(EDGE + 1 + off, 1), :]
    rot[...] = jnp.broadcast_to(turn * share, (128, 128)).T

    def down(j, carry):
        last, e, kc = carry
        tile_in(j).wait()
        flat = inp.at[j].reshape(CELLS * 8, 128)
        kr = pltpu.roll(kbuf[...], lax.rem(128 - 8 * j, 128), 1)
        for p in range(8):
            kn = jnp.broadcast_to(kr[:, p + 1 : p + 2], (CELLS, 128))
            g = 1.0 + kc * e
            inv = 1.0 / (g + kn)
            last = (flat[pl.ds(p, CELLS, stride=8), :] + kc * last) * inv
            e = g * inv
            dp[j, p] = last
            cp[j, p] = kn * inv
            kc = kn
        return last, e, kc

    zero = jnp.zeros((CELLS, 128), jnp.float32)
    lax.fori_loop(
        0, TILES, down, (zero, zero + 1.0, jnp.broadcast_to(kbuf[:, 0:1], (CELLS, 128)))
    )

    @pl.when(has_south & has_north)
    def _():
        pl.semaphore_wait(barrier, PEERS + 2)

    @pl.when(jnp.logical_not(has_south & has_north))
    def _():
        pl.semaphore_wait(barrier, PEERS + 1)

    def up(c, x):
        j = TILES - 1 - c
        for p in reversed(range(8)):
            x = dp[j, p] + cp[j, p] * x
            dp[j, p] = x
        for d in range(1, PEERS):
            to = (me + d) % PEERS
            forth(j, to, me, to).start()
        pltpu.make_async_copy(dp.at[j, me], got.at[j, me], fr.at[j, me]).start()
        return x

    lax.fori_loop(0, TILES, up, zero)

    def gather(j):
        for d in range(1, PEERS):
            s = (me + d) % PEERS
            forth(j, s, s, s).wait_recv()
        pltpu.make_async_copy(dp.at[j, me], got.at[j, me], fr.at[j, me]).wait()
        for s in range(PEERS):
            circ[j, LEFT + CELLS * s : LEFT + CELLS * (s + 1), :] = got[j, s]
        begin = jnp.clip(LEFT + (off + 1) * (HALF - EDGE), LEFT, RIGHT - EDGE)
        edge[j] = circ[j, pl.ds(begin, EDGE), :]
        edge_copy(j).start()
        field = circ[j, LEFT:RIGHT, :]
        high = field.astype(jnp.bfloat16)
        low = (field - high.astype(jnp.float32)).astype(jnp.bfloat16)
        part = jnp.dot(
            project_ref[...], jnp.concatenate([high, low], axis=1), preferred_element_type=jnp.float32
        )
        n = 2 * KPAD
        spec[j] = part[:n, :128] + part[n:, :128] + part[:n, 128:]
        spec_copy(j).start()

    def filt(j):
        edge_copy(j).wait_recv()
        taken = edge_in[j]
        circ[j, 0:EDGE, :] = taken
        circ[j, RIGHT : RIGHT + EDGE, :] = taken
        spec_copy(j).wait_recv()
        level = lax.broadcasted_iota(jnp.int32, (KPAD, 128), 0)
        sign = jnp.where(level % 2 == 0, 1.0, -1.0)
        a = spec[j, 0:KPAD, :] + sign * spec_in[j, 0:KPAD, :]
        b = spec[j, KPAD : 2 * KPAD, :] + sign * spec_in[j, KPAD : 2 * KPAD, :]
        c = rot[0:KPAD, :]
        d = rot[KPAD : 2 * KPAD, :]
        turned = jnp.concatenate([c * a - d * b, d * a + c * b], axis=0)
        high = turned.astype(jnp.bfloat16)
        low = (turned - high.astype(jnp.float32)).astype(jnp.bfloat16)
        weight = jnp.concatenate(
            [
                jnp.concatenate([high, low], axis=1),
                jnp.concatenate([high, jnp.zeros_like(low)], axis=1),
            ],
            axis=0,
        )
        block = HALF // 3
        for s in range(3):
            lowpass = jnp.dot(
                rebuild_ref[s * block : (s + 1) * block, :], weight, preferred_element_type=jnp.float32
            )
            near = circ[j, pl.ds(LEFT + s * block - off, block), :]
            far = circ[j, pl.ds(LEFT + s * block - 1 - off, block), :]
            moved = (1.0 - frac) * near + frac * far
            rows[2, j, s * block : (s + 1) * block, :] = (
                keep * moved + lowpass[:, :128] + lowpass[:, 128:]
            )

        @pl.when(has_north)
        def _():
            row_copy(j, 0, lat + 1).start()

        @pl.when(has_south)
        def _():
            row_copy(j, 1, lat - 1).start()

    south_slot = jnp.where(has_south, 0, 2)
    north_slot = jnp.where(has_north, 1, 2)

    def spread(j):
        @pl.when(has_south)
        def _():
            row_copy(j, 0, lat - 1).wait_recv()

        @pl.when(has_north)
        def _():
            row_copy(j, 1, lat + 1).wait_recv()

        for s in range(PEERS):
            part = pl.ds(CELLS * s, CELLS)
            got[j, s] = (1.0 - 2.0 * mix) * rows[2, j, part, :] + mix * (
                rows[south_slot, j, part, :] + rows[north_slot, j, part, :]
            )
        for d in range(1, PEERS):
            to = (me + d) % PEERS
            home(j, to, me, to).start()
        pltpu.make_async_copy(got.at[j, me], back.at[j, me], br.at[j, me]).start()

    def finish(j):
        for d in range(1, PEERS):
            s = (me + d) % PEERS
            home(j, s, s, s).wait_recv()
        pltpu.make_async_copy(got.at[j, me], back.at[j, me], br.at[j, me]).wait()
        flat = outb.at[j].reshape(CELLS * 8, 128)
        light = glow[...]
        for p in range(PEERS):
            level = j * 8 + p
            top = back[j, p] + source_ref[pl.ds(level, 1), :] * light
            flat[pl.ds(p, CELLS, stride=8), :] = top / (1.0 + loss_ref[pl.ds(level, 1), :] * light)
        tile_out(j).start()

    stages = ((gather, 0), (filt, 1), (spread, 3), (finish, 4))

    def step(t, carry):
        for stage, lag in stages:

            @pl.when((t >= lag) & (t < lag + TILES))
            def _():
                stage(TILES - 1 - (t - lag))

        return carry

    lax.fori_loop(0, TILES + stages[-1][1], step, 0)

    def drain(j, carry):
        for d in range(1, PEERS):
            to = (me + d) % PEERS
            forth(j, to, me, to).wait_send()
            home(j, to, me, to).wait_send()
        edge_copy(j).wait_send()
        spec_copy(j).wait_send()

        @pl.when(has_north)
        def _():
            row_copy(j, 0, lat + 1).wait_send()

        @pl.when(has_south)
        def _():
            row_copy(j, 1, lat - 1).wait_send()

        tile_out(j).wait()
        return carry

    lax.fori_loop(0, TILES, drain, 0)


def body(tracers, offsets, fraction, cutoffs, keep_high, mixing, kz, light, loss_rate, source):
    project, rebuild, turn = wave_tables()
    levels, species = tracers.shape[2:]
    smem = pl.BlockSpec(memory_space=pltpu.SMEM)
    vmem = pl.BlockSpec(memory_space=pltpu.VMEM)
    hbm = pl.BlockSpec(memory_space=pl.ANY)
    f32 = jnp.float32
    dma = pltpu.SemaphoreType.DMA
    out = pl.pallas_call(
        kernel,
        out_shape=jax.ShapeDtypeStruct((CELLS, levels, species), f32),
        in_specs=[smem] * 6 + [hbm] + [vmem] * 6,
        out_specs=hbm,
        scratch_shapes=[
            pltpu.VMEM((TILES, CELLS, 8, 128), f32),
            pltpu.VMEM((CELLS, 128), f32),
            pltpu.VMEM((CELLS, 128), f32),
            pltpu.VMEM((128, 128), f32),
            pltpu.VMEM((TILES, PEERS, CELLS, 128), f32),
            pltpu.VMEM((TILES, PEERS, CELLS, 128), f32),
            pltpu.VMEM((TILES, PEERS, CELLS, 128), f32),
            pltpu.VMEM((TILES, HALF + 2 * EDGE, 128), f32),
            pltpu.VMEM((TILES, EDGE, 128), f32),
            pltpu.VMEM((TILES, EDGE, 128), f32),
            pltpu.VMEM((TILES, 2 * KPAD, 128), f32),
            pltpu.VMEM((TILES, 2 * KPAD, 128), f32),
            pltpu.VMEM((3, TILES, HALF, 128), f32),
            pltpu.VMEM((TILES, PEERS, CELLS, 128), f32),
            pltpu.VMEM((TILES, CELLS, 8, 128), f32),
            dma((TILES,)),
            dma((TILES, PEERS)),
            dma((TILES, PEERS)),
            dma((TILES,)),
            dma((TILES,)),
            dma((TILES,)),
            dma((TILES,)),
            dma((2, TILES)),
            dma((2, TILES)),
            dma((TILES, PEERS)),
            dma((TILES, PEERS)),
            dma((TILES,)),
        ],
        compiler_params=pltpu.CompilerParams(
            collective_id=0, has_side_effects=True, vmem_limit_bytes=58 << 20
        ),
        name="transport",
    )(
        offsets,
        fraction,
        cutoffs,
        keep_high,
        mixing,
        light,
        tracers.reshape(CELLS, levels, species),
        kz.reshape(CELLS, levels),
        loss_rate,
        source,
        jnp.asarray(project),
        jnp.asarray(rebuild),
        jnp.asarray(turn),
    )
    return out.reshape(tracers.shape)


def solution(mesh):
    return jax.shard_map(
        body,
        mesh=mesh,
        in_specs=(
            P("lat", "lon", None, None),
            P("lat"),
            P("lat"),
            P("lat"),
            P("lat"),
            P("lat"),
            P("lat", "lon", None),
            P("lat", "lon"),
            P(),
            P(),
        ),
        out_specs=P("lat", "lon", None, None),
        check_vma=False,
    )
```

time: 499 us -> 180 us (0.36); the launches traced: 490 us -> 178 us
  waiting for transfers between devices: 305 us -> 0 us
  Pallas kernels: 0 us -> 169 us
  other arithmetic: 84.3 us -> 0 us
  local copies, waits for them, and re-layouts: 49.3 us -> 5.36 us
  starting transfers between devices: 18.1 us -> 0 us
  matrix products: 14.9 us -> 0 us
  between operations: 17.1 us -> 3.24 us
    ppermute x7 -> x0, waiting for transfers between devices: 176 us -> none  [the longest x5 107 us: passed_along(): lax.ppermute(array, axis, [(i, (i + by) % count) for i in range(count)])]
    pallas_call x0 -> x1, Pallas kernels: none -> 169 us  [body(): pl.pallas_call(kernel, out_shape=jax.ShapeDtypeStruct((CELLS, levels, spe...]
    psum x1 -> x0, waiting for transfers between devices: 130 us -> none  [body(): spectra = lax.psum(project(table, moved), 'lon')]
    while x152 -> x0, other arithmetic: 51 us -> none
    ppermute x7 -> x0, starting transfers between devices: 18.1 us -> none  [the longest x5 11.2 us: passed_along(): lax.ppermute(array, axis, [(i, (i + by) % count) for i in range(count)])]
    dot_general x2 -> x0, matrix products: 14.9 us -> none  [the longest x1 8.76 us: rebuild(): jnp.einsum('ik,rkf->rif', table, spectra * weights[:, :, None], precision...]
    concatenate x4 -> x0, local copies, waits for them, and re-layouts: 11 us -> none  [column_solve(): lax.linalg.tridiagonal_solve(below, 1.0 + coupling + above, -above, field)]
    select_n x2 -> x0, other arithmetic: 8.52 us -> none  [the longest x1 8.51 us: body(): upper_block = jnp.where(chosen(-quotient == distance), western, upper_block)]
  transfers between devices with their start and end apart: 8 -> 0, of which waited for: 7 -> 0; matrix products, arithmetic and copies ran while one was open for 0% -> 0% of each run, Pallas kernels for 0% -> 0%
where the time goes in v1:
time: 180 us; the launch traced here: 178 us
  Pallas kernels  169 us (94%)
  local copies, waits for them, and re-layouts  5.36 us (3%)
  between operations  3.24 us (2%)
    pallas_call x1, Pallas kernels, body(): pl.pallas_call(kernel, out_shape=jax.ShapeDtypeStruct((CELLS, levels, spe...  169 us
    unnamed x2, local copies, waits for them, and re-layouts  5.36 us

profile of v1, /device:TPU:87, one launch (start us, length us, event | category | flops | bytes accessed | tf_op | source)
XLA Modules:
  0.0 177.9 jit_solution(15918669115098178630)
XLA Ops:
  3.2 1.5 copy.14
  4.7 169.3 %transport.1 = f32[90,72,128]{2,1,0:T(8,128)} custom-call(s32[1]{0:T(128)S(6)} %copy.16.off_ref, f32[1]{0:T(128)S(6)} %copy.17.frac_ref, s32[1]{0:T(128)S(6)} %copy.18.cut_ref, f32[1]{0:T(128)S(6)} %copy.19.keep_ref, f32[1]{0:T(128)S(6)} %copy.20.mix_ref, f32[1,90]{1,0:T(1,128)} %light_ref.1, f32[90,72,128]{2,1,0:T(8,128)} %bitcast.4, f32[90,72]{1,0:T(8,128)} %bitcast.5, ...), custom_call_target="tpu_custom_call" | custom-call | tf_op jit(solution)/shard_map/transport/pallas_call | solution.py:369
  174.0 3.9 %copy.21 = f32[1,90,72,128]{3,2,1,0:T(8,128)} copy(f32[1,90,72,128]{3,2,1,0:T(8,128)} %bitcast.3) | data formatting | bytes 6635520

commit v2 on v1

--- a/solution.py
+++ b/solution.py
@@ -18,6 +18,8 @@
 TILES = 9
 EDGE = 184
 KPAD = 56
+DIRECT = 360
+RELAYED = ((3, 7), (7, 3), (7, 4), (4, 7), (4, 0), (0, 4), (0, 3), (3, 0))
 LEFT = EDGE
 RIGHT = EDGE + HALF
 
@@ -76,6 +78,7 @@
     spec,
     spec_in,
     rows,
+    relay,
     back,
     outb,
     in_sem,
@@ -87,6 +90,10 @@
     sr,
     ls,
     lr,
+    rs,
+    rr,
+    os,
+    orr,
     bs,
     br,
     out_sem,
@@ -98,6 +105,8 @@
     other = {"lon": (lon + PEERS) % (2 * PEERS), "lat": lat}
     has_south = lat > 0
     has_north = lat < 7
+    plain_south = has_south & (lat != 4)
+    plain_north = has_north & (lat != 3)
 
     def peer(p):
         return {"lon": base + p, "lat": lat}
@@ -139,6 +148,25 @@
     def row_copy(j, slot, to):
         return pltpu.make_async_remote_copy(
             rows.at[2, j], rows.at[slot, j], ls.at[slot, j], lr.at[slot, j],
+            device_id={"lon": lon, "lat": to}, device_id_type=MESH,
+        )
+
+    def half_copy(j, slot, to):
+        return pltpu.make_async_remote_copy(
+            rows.at[2, j, pl.ds(0, DIRECT)], rows.at[slot, j, pl.ds(0, DIRECT)],
+            ls.at[slot, j], lr.at[slot, j],
+            device_id={"lon": lon, "lat": to}, device_id_type=MESH,
+        )
+
+    def relay_copy(j, to):
+        return pltpu.make_async_remote_copy(
+            rows.at[2, j, pl.ds(DIRECT, HALF - DIRECT)], relay.at[j], rs.at[j], rr.at[j],
+            device_id={"lon": lon, "lat": to}, device_id_type=MESH,
+        )
+
+    def onward_copy(j, slot, to):
+        return pltpu.make_async_remote_copy(
+            relay.at[j], rows.at[slot, j, pl.ds(DIRECT, HALF - DIRECT)], os.at[j], orr.at[j],
             device_id={"lon": lon, "lat": to}, device_id_type=MESH,
         )
 
@@ -165,12 +193,21 @@
             barrier, inc=1, device_id={"lon": lon, "lat": lat + 1}, device_id_type=MESH
         )
 
+    for here, there in RELAYED:
+
+        @pl.when(lat == here)
+        def _():
+            pl.semaphore_signal(
+                barrier, inc=1, device_id={"lon": lon, "lat": there}, device_id_type=MESH
+            )
+
     off = off_ref[0]
     frac = frac_ref[0]
     keep = keep_ref[0]
     mix = mix_ref[0]
-    kbuf[...] = jnp.zeros_like(kbuf)
-    kbuf[:, 0:72] = kz_ref[...]
+    rot[...] = jnp.zeros_like(rot)
+    rot[0:72, 0:CELLS] = kz_ref[...]
+    kbuf[...] = rot[...].T[0:CELLS, :]
 
     def light_row(c, carry):
         glow[pl.ds(c, 1), :] = jnp.full((1, 128), light_ref[0, c], jnp.float32)
@@ -205,24 +242,38 @@
         0, TILES, down, (zero, zero + 1.0, jnp.broadcast_to(kbuf[:, 0:1], (CELLS, 128)))
     )
 
-    @pl.when(has_south & has_north)
+    edge_row = (lat == 0) | (lat == 7)
+    cross_row = (lat == 3) | (lat == 4)
+
+    @pl.when(edge_row)
+    def _():
+        pl.semaphore_wait(barrier, PEERS + 3)
+
+    @pl.when(cross_row)
+    def _():
+        pl.semaphore_wait(barrier, PEERS + 4)
+
+    @pl.when(jnp.logical_not(edge_row | cross_row))
     def _():
         pl.semaphore_wait(barrier, PEERS + 2)
-
-    @pl.when(jnp.logical_not(has_south & has_north))
-    def _():
-        pl.semaphore_wait(barrier, PEERS + 1)
 
     def up(c, x):
         j = TILES - 1 - c
         for p in reversed(range(8)):
             x = dp[j, p] + cp[j, p] * x
             dp[j, p] = x
+
+        @pl.when(c == 0)
+        def _():
+            send(j)
+
+        return x
+
+    def send(j):
         for d in range(1, PEERS):
             to = (me + d) % PEERS
             forth(j, to, me, to).start()
         pltpu.make_async_copy(dp.at[j, me], got.at[j, me], fr.at[j, me]).start()
-        return x
 
     lax.fori_loop(0, TILES, up, zero)
 
@@ -231,6 +282,15 @@
             s = (me + d) % PEERS
             forth(j, s, s, s).wait_recv()
         pltpu.make_async_copy(dp.at[j, me], got.at[j, me], fr.at[j, me]).wait()
+
+        @pl.when(j == TILES - 1)
+        def _():
+            send(j - 1)
+
+        @pl.when(j >= 2)
+        def _():
+            send(j - 2)
+
         for s in range(PEERS):
             circ[j, LEFT + CELLS * s : LEFT + CELLS * (s + 1), :] = got[j, s]
         begin = jnp.clip(LEFT + (off + 1) * (HALF - EDGE), LEFT, RIGHT - EDGE)
@@ -280,25 +340,56 @@
                 keep * moved + lowpass[:, :128] + lowpass[:, 128:]
             )
 
-        @pl.when(has_north)
+        @pl.when(lat == 3)
+        def _():
+            half_copy(j, 0, 4).start()
+            relay_copy(j, 7).start()
+
+        @pl.when(lat == 4)
+        def _():
+            half_copy(j, 1, 3).start()
+            relay_copy(j, 0).start()
+
+        @pl.when(plain_north)
         def _():
             row_copy(j, 0, lat + 1).start()
 
-        @pl.when(has_south)
+        @pl.when(plain_south)
         def _():
             row_copy(j, 1, lat - 1).start()
+
+    def onward(j):
+        @pl.when(lat == 7)
+        def _():
+            relay_copy(j, 7).wait_recv()
+            onward_copy(j, 0, 4).start()
+
+        @pl.when(lat == 0)
+        def _():
+            relay_copy(j, 0).wait_recv()
+            onward_copy(j, 1, 3).start()
 
     south_slot = jnp.where(has_south, 0, 2)
     north_slot = jnp.where(has_north, 1, 2)
 
     def spread(j):
-        @pl.when(has_south)
+        @pl.when(plain_south)
         def _():
             row_copy(j, 0, lat - 1).wait_recv()
 
-        @pl.when(has_north)
+        @pl.when(plain_north)
         def _():
             row_copy(j, 1, lat + 1).wait_recv()
+
+        @pl.when(lat == 4)
+        def _():
+            half_copy(j, 0, 3).wait_recv()
+            onward_copy(j, 0, 7).wait_recv()
+
+        @pl.when(lat == 3)
+        def _():
+            half_copy(j, 1, 4).wait_recv()
+            onward_copy(j, 1, 0).wait_recv()
 
         for s in range(PEERS):
             part = pl.ds(CELLS * s, CELLS)
@@ -323,7 +414,7 @@
             flat[pl.ds(p, CELLS, stride=8), :] = top / (1.0 + loss_ref[pl.ds(level, 1), :] * light)
         tile_out(j).start()
 
-    stages = ((gather, 0), (filt, 1), (spread, 3), (finish, 4))
+    stages = ((filt, 2), (onward, 3), (gather, 0), (finish, 4), (spread, 3))
 
     def step(t, carry):
         for stage, lag in stages:
@@ -334,7 +425,7 @@
 
         return carry
 
-    lax.fori_loop(0, TILES + stages[-1][1], step, 0)
+    lax.fori_loop(0, TILES + 4, step, 0)
 
     def drain(j, carry):
         for d in range(1, PEERS):
@@ -344,13 +435,31 @@
         edge_copy(j).wait_send()
         spec_copy(j).wait_send()
 
-        @pl.when(has_north)
+        @pl.when(plain_north)
         def _():
             row_copy(j, 0, lat + 1).wait_send()
 
-        @pl.when(has_south)
+        @pl.when(plain_south)
         def _():
             row_copy(j, 1, lat - 1).wait_send()
+
+        @pl.when(lat == 3)
+        def _():
+            half_copy(j, 0, 4).wait_send()
+            relay_copy(j, 7).wait_send()
+
+        @pl.when(lat == 4)
+        def _():
+            half_copy(j, 1, 3).wait_send()
+            relay_copy(j, 0).wait_send()
+
+        @pl.when(lat == 7)
+        def _():
+            onward_copy(j, 0, 4).wait_send()
+
+        @pl.when(lat == 0)
+        def _():
+            onward_copy(j, 1, 3).wait_send()
 
         tile_out(j).wait()
         return carry
@@ -385,6 +494,7 @@
             pltpu.VMEM((TILES, 2 * KPAD, 128), f32),
             pltpu.VMEM((TILES, 2 * KPAD, 128), f32),
             pltpu.VMEM((3, TILES, HALF, 128), f32),
+            pltpu.VMEM((TILES, HALF - DIRECT, 128), f32),
             pltpu.VMEM((TILES, PEERS, CELLS, 128), f32),
             pltpu.VMEM((TILES, CELLS, 8, 128), f32),
             dma((TILES,)),
@@ -396,6 +506,10 @@
             dma((TILES,)),
             dma((2, TILES)),
             dma((2, TILES)),
+            dma((TILES,)),
+            dma((TILES,)),
+            dma((TILES,)),
+            dma((TILES,)),
             dma((TILES, PEERS)),
             dma((TILES, PEERS)),
             dma((TILES,)),
@@ -412,7 +526,7 @@
         mixing,
         light,
         tracers.reshape(CELLS, levels, species),
-        kz.reshape(CELLS, levels),
+        kz.reshape(CELLS, levels).T,
         loss_rate,
         source,
         jnp.asarray(project),

time: 180 us -> 118 us (0.66)
  the two profiles are of different devices: /device:TPU:87 before, /device:TPU:25 now
where the time goes in v2:
time: 118 us
  Pallas kernels  111 us (94%)
  local copies, waits for them, and re-layouts  3.87 us (3%)
  between operations  3.24 us (3%)
    pallas_call x1, Pallas kernels, body(): pl.pallas_call(kernel, out_shape=jax.ShapeDtypeStruct((CELLS, levels, spe...  111 us
    unnamed x1, local copies, waits for them, and re-layouts  3.87 us

profile of v2, /device:TPU:25, one launch (start us, length us, event | category | flops | bytes accessed | tf_op | source)
XLA Modules:
  0.0 117.9 jit_solution(16224604771826180987)
XLA Ops:
  3.2 110.8 %transport.1 = f32[90,72,128]{2,1,0:T(8,128)} custom-call(s32[1]{0:T(128)S(6)} %copy.15.off_ref, f32[1]{0:T(128)S(6)} %copy.16.frac_ref, s32[1]{0:T(128)S(6)} %copy.17.cut_ref, f32[1]{0:T(128)S(6)} %copy.18.keep_ref, f32[1]{0:T(128)S(6)} %copy.19.mix_ref, f32[1,90]{1,0:T(1,128)} %light_ref.1, f32[90,72,128]{2,1,0:T(8,128)} %bitcast.6, f32[72,90]{1,0:T(8,128)} %bitcast.7, ...), custom_call_target="tpu_custom_call" | custom-call | tf_op jit(solution)/shard_map/transport/pallas_call | solution.py:478
  114.0 3.9 %copy.20 = f32[1,90,72,128]{3,2,1,0:T(8,128)} copy(f32[1,90,72,128]{3,2,1,0:T(8,128)} %bitcast.5) | data formatting | bytes 6635520

commit v3 on v2

v3 whole, which is shorter than its diff:
```python
import functools
import math

import jax
import jax.numpy as jnp
import numpy as np
from jax import lax
from jax.experimental import pallas as pl
from jax.experimental.pallas import tpu as pltpu
from jax.sharding import PartitionSpec as P

NLON = 1440
KMAX = 48
MESH = pl.DeviceIdType.MESH
CELLS = 90
PEERS = 8
HALF = CELLS * PEERS
LEVELS = 72
TILES = 9
EDGE = 184
KPAD = 56
DIRECT = HALF // 2
GROUP = PEERS // 2
RELAYED = ((3, 7), (7, 3), (7, 4), (4, 7), (4, 0), (0, 4), (0, 3), (3, 0))
LEFT = EDGE
RIGHT = EDGE + HALF


def split_bf16(table):
    import ml_dtypes

    high = table.astype(ml_dtypes.bfloat16)
    low = (table - high.astype(np.float64)).astype(ml_dtypes.bfloat16)
    return high, low


def wave_tables():
    places = np.arange(HALF)
    waves = np.arange(KMAX + 1)
    phase = (places[:, None] * waves[None, :] % NLON) * (2.0 * math.pi / NLON)
    table = np.zeros((HALF, 2 * KPAD))
    table[:, : KMAX + 1] = np.cos(phase)
    table[:, KPAD : KPAD + KMAX + 1] = np.sin(phase)
    high, low = split_bf16(table)
    rebuild = np.concatenate([high, low], axis=1)
    project = np.ascontiguousarray(rebuild.T)
    shifts = np.arange(-EDGE, EDGE)
    phase = (shifts[:, None] * waves[None, :] % NLON) * (2.0 * math.pi / NLON)
    turn = np.zeros((2 * EDGE, 128), np.float32)
    turn[:, : KMAX + 1] = np.cos(phase)
    turn[:, KPAD : KPAD + KMAX + 1] = np.sin(phase)
    return project, rebuild, turn


def kernel(
    off_hbm,
    frac_hbm,
    cut_hbm,
    keep_hbm,
    mix_hbm,
    light_hbm,
    tracers_ref,
    kz_hbm,
    turn_hbm,
    project_hbm,
    rebuild_hbm,
    loss_hbm,
    source_hbm,
    out_ref,
    off_ref,
    frac_ref,
    cut_ref,
    keep_ref,
    mix_ref,
    light_ref,
    kz_ref,
    turn_ref,
    project_ref,
    rebuild_ref,
    loss_ref,
    source_ref,
    inp,
    kbuf,
    glow,
    rot,
    dp,
    cp,
    got,
    circ,
    given,
    taken,
    rows,
    relay,
    back,
    in_sem,
    fs,
    fr,
    es,
    ss,
    er,
    ls,
    lr,
    rs,
    rr,
    os,
    bs,
    br,
    arg_sem,
):
    lon = lax.axis_index("lon")
    lat = lax.axis_index("lat")
    me = lon % PEERS
    base = lon - me
    other = {"lon": (lon + PEERS) % (2 * PEERS), "lat": lat}
    has_south = lat > 0
    has_north = lat < 7
    plain_south = has_south & (lat != 4)
    plain_north = has_north & (lat != 3)

    def peer(p):
        return {"lon": base + p, "lat": lat}

    def tile_in(j):
        return pltpu.make_async_copy(
            tracers_ref.at[:, pl.ds(pl.multiple_of(j * 8, 8), 8), :], inp.at[j], in_sem.at[j]
        )

    def forth(j, src, dst, to):
        return pltpu.make_async_remote_copy(
            dp.at[j, src], got.at[j, dst], fs, fr.at[j], device_id=peer(to), device_id_type=MESH
        )

    def home(j, src, dst, to):
        return pltpu.make_async_remote_copy(
            got.at[j, src], back.at[j, dst], bs, br.at[j], device_id=peer(to), device_id_type=MESH
        )

    def edge_copy(j):
        return pltpu.make_async_remote_copy(
            given.at[j, pl.ds(0, EDGE)], taken.at[j, pl.ds(0, EDGE)], es, er.at[j],
            device_id=other, device_id_type=MESH,
        )

    def spec_copy(j):
        return pltpu.make_async_remote_copy(
            given.at[j, pl.ds(EDGE, 2 * KPAD)], taken.at[j, pl.ds(EDGE, 2 * KPAD)], ss, er.at[j],
            device_id=other, device_id_type=MESH,
        )

    def half(h):
        return pl.ds(h * DIRECT, DIRECT)

    def row_copy(j, h, slot, to):
        return pltpu.make_async_remote_copy(
            rows.at[2, j, half(h)], rows.at[slot, j, half(h)], ls.at[slot], lr.at[slot, h, j],
            device_id={"lon": lon, "lat": to}, device_id_type=MESH,
        )

    def relay_copy(j, to):
        return pltpu.make_async_remote_copy(
            rows.at[2, j, half(1)], relay.at[j], rs, rr.at[j],
            device_id={"lon": lon, "lat": to}, device_id_type=MESH,
        )

    def onward_copy(j, slot, to):
        return pltpu.make_async_remote_copy(
            relay.at[j], rows.at[slot, j, half(1)], os, lr.at[slot, 1, j],
            device_id={"lon": lon, "lat": to}, device_id_type=MESH,
        )

    def start_in(j, carry):
        tile_in(j).start()
        return carry

    pairs = (
        (kz_hbm, kz_ref),
        (off_hbm, off_ref),
        (frac_hbm, frac_ref),
        (cut_hbm, cut_ref),
        (keep_hbm, keep_ref),
        (mix_hbm, mix_ref),
        (light_hbm, light_ref),
        (turn_hbm, turn_ref),
        (project_hbm, project_ref),
        (rebuild_hbm, rebuild_ref),
        (loss_hbm, loss_ref),
        (source_hbm, source_ref),
    )
    arrivals = [
        pltpu.make_async_copy(src, dst, arg_sem.at[n]) for n, (src, dst) in enumerate(pairs)
    ]
    arrivals[0].start()
    lax.fori_loop(0, TILES, start_in, 0)
    for copy in arrivals[1:]:
        copy.start()

    barrier = pltpu.get_barrier_semaphore()
    for d in range(1, PEERS):
        pl.semaphore_signal(barrier, inc=1, device_id=peer((me + d) % PEERS), device_id_type=MESH)
    pl.semaphore_signal(barrier, inc=1, device_id=other, device_id_type=MESH)

    @pl.when(has_south)
    def _():
        pl.semaphore_signal(
            barrier, inc=1, device_id={"lon": lon, "lat": lat - 1}, device_id_type=MESH
        )

    @pl.when(has_north)
    def _():
        pl.semaphore_signal(
            barrier, inc=1, device_id={"lon": lon, "lat": lat + 1}, device_id_type=MESH
        )

    for here, there in RELAYED:

        @pl.when(lat == here)
        def _():
            pl.semaphore_signal(
                barrier, inc=1, device_id={"lon": lon, "lat": there}, device_id_type=MESH
            )

    arrivals[0].wait()
    rot[...] = jnp.zeros_like(rot)
    rot[0:72, 0:CELLS] = kz_ref[...]
    kbuf[...] = rot[...].T[0:CELLS, :]

    def down(j, carry):
        last, e, kc = carry
        tile_in(j).wait()
        flat = inp.at[j].reshape(CELLS * 8, 128)
        kr = pltpu.roll(kbuf[...], lax.rem(128 - 8 * j, 128), 1)
        for p in range(8):
            kn = jnp.broadcast_to(kr[:, p + 1 : p + 2], (CELLS, 128))
            g = 1.0 + kc * e
            inv = 1.0 / (g + kn)
            last = (flat[pl.ds(p, CELLS, stride=8), :] + kc * last) * inv
            e = g * inv
            dp[j, p] = last
            cp[j, p] = kn * inv
            kc = kn
        return last, e, kc

    zero = jnp.zeros((CELLS, 128), jnp.float32)
    lax.fori_loop(
        0, TILES, down, (zero, zero + 1.0, jnp.broadcast_to(kbuf[:, 0:1], (CELLS, 128)))
    )

    edge_row = (lat == 0) | (lat == 7)
    cross_row = (lat == 3) | (lat == 4)

    @pl.when(edge_row)
    def _():
        pl.semaphore_wait(barrier, PEERS + 3)

    @pl.when(cross_row)
    def _():
        pl.semaphore_wait(barrier, PEERS + 4)

    @pl.when(jnp.logical_not(edge_row | cross_row))
    def _():
        pl.semaphore_wait(barrier, PEERS + 2)

    def up(c, x):
        j = TILES - 1 - c
        for p in reversed(range(8)):
            x = dp[j, p] + cp[j, p] * x
            dp[j, p] = x

        @pl.when(c == 0)
        def _():
            send(j)

        return x

    def send(j):
        for d in range(1, PEERS):
            to = (me + d) % PEERS
            forth(j, to, me, to).start()
        pltpu.make_async_copy(dp.at[j, me], got.at[j, me], fr.at[j]).start()

    lax.fori_loop(0, TILES, up, zero)

    for copy in arrivals[1:]:
        copy.wait()
    off = off_ref[0]
    frac = frac_ref[0]
    keep = keep_ref[0]
    mix = mix_ref[0]

    def light_row(c, carry):
        glow[pl.ds(c, 1), :] = jnp.full((1, 128), light_ref[0, c], jnp.float32)
        return carry

    lax.fori_loop(0, CELLS, light_row, 0)

    lane = lax.broadcasted_iota(jnp.int32, (1, 128), 1)
    wave = lane % KPAD
    share = jnp.where(wave <= cut_ref[0], jnp.where(wave == 0, 1.0, 2.0) / NLON, 0.0) * (1.0 - keep)
    turn = (1.0 - frac) * turn_ref[pl.ds(EDGE + off, 1), :] + frac * turn_ref[pl.ds(EDGE + 1 + off, 1), :]
    rot[...] = jnp.broadcast_to(turn * share, (128, 128)).T

    def gather(j):
        pltpu.make_async_copy(dp.at[j], got.at[j], fr.at[j]).wait()

        @pl.when(j == TILES - 1)
        def _():
            send(j - 1)

        @pl.when(j >= 2)
        def _():
            send(j - 2)

        for s in range(PEERS):
            circ[j, LEFT + CELLS * s : LEFT + CELLS * (s + 1), :] = got[j, s]
        begin = jnp.clip(LEFT + (off + 1) * (HALF - EDGE), LEFT, RIGHT - EDGE)
        given[j, 0:EDGE, :] = circ[j, pl.ds(begin, EDGE), :]
        edge_copy(j).start()
        field = circ[j, LEFT:RIGHT, :]
        high = field.astype(jnp.bfloat16)
        low = (field - high.astype(jnp.float32)).astype(jnp.bfloat16)
        part = jnp.dot(
            project_ref[...], jnp.concatenate([high, low], axis=1), preferred_element_type=jnp.float32
        )
        n = 2 * KPAD
        given[j, EDGE : EDGE + n, :] = part[:n, :128] + part[n:, :128] + part[:n, 128:]
        spec_copy(j).start()

    def filt(j):
        pltpu.make_async_copy(given.at[j], taken.at[j], er.at[j]).wait()
        fresh = taken[j, 0:EDGE, :]
        circ[j, 0:EDGE, :] = fresh
        circ[j, RIGHT : RIGHT + EDGE, :] = fresh
        level = lax.broadcasted_iota(jnp.int32, (KPAD, 128), 0)
        sign = jnp.where(level % 2 == 0, 1.0, -1.0)
        cosine, sine = slice(EDGE, EDGE + KPAD), slice(EDGE + KPAD, EDGE + 2 * KPAD)
        a = given[j, cosine, :] + sign * taken[j, cosine, :]
        b = given[j, sine, :] + sign * taken[j, sine, :]
        c = rot[0:KPAD, :]
        d = rot[KPAD : 2 * KPAD, :]
        turned = jnp.concatenate([c * a - d * b, d * a + c * b], axis=0)
        high = turned.astype(jnp.bfloat16)
        low = (turned - high.astype(jnp.float32)).astype(jnp.bfloat16)
        weight = jnp.concatenate(
            [
                jnp.concatenate([high, low], axis=1),
                jnp.concatenate([high, jnp.zeros_like(low)], axis=1),
            ],
            axis=0,
        )
        for h in range(2):
            first = h * DIRECT
            lowpass = jnp.dot(
                rebuild_ref[first : first + DIRECT, :], weight, preferred_element_type=jnp.float32
            )
            near = circ[j, pl.ds(LEFT + first - off, DIRECT), :]
            far = circ[j, pl.ds(LEFT + first - 1 - off, DIRECT), :]
            moved = (1.0 - frac) * near + frac * far
            rows[2, j, first : first + DIRECT, :] = keep * moved + lowpass[:, :128] + lowpass[:, 128:]

            @pl.when(plain_north)
            def _():
                row_copy(j, h, 0, lat + 1).start()

            @pl.when(plain_south)
            def _():
                row_copy(j, h, 1, lat - 1).start()

            @pl.when(lat == 3)
            def _():
                (relay_copy(j, 7) if h else row_copy(j, 0, 0, 4)).start()

            @pl.when(lat == 4)
            def _():
                (relay_copy(j, 0) if h else row_copy(j, 0, 1, 3)).start()

    def onward(j):
        @pl.when(lat == 7)
        def _():
            relay_copy(j, 7).wait_recv()
            onward_copy(j, 0, 4).start()

        @pl.when(lat == 0)
        def _():
            relay_copy(j, 0).wait_recv()
            onward_copy(j, 1, 3).start()

    south_slot = jnp.where(has_south, 0, 2)
    north_slot = jnp.where(has_north, 1, 2)

    def spread(j):
        for h in range(2):

            @pl.when(has_south)
            def _():
                row_copy(j, h, 0, lat - 1).wait_recv()

            @pl.when(has_north)
            def _():
                row_copy(j, h, 1, lat + 1).wait_recv()

            for s in range(h * GROUP, (h + 1) * GROUP):
                part = pl.ds(CELLS * s, CELLS)
                got[j, s] = (1.0 - 2.0 * mix) * rows[2, j, part, :] + mix * (
                    rows[south_slot, j, part, :] + rows[north_slot, j, part, :]
                )
            for d in range(1, GROUP):
                to = h * GROUP + (me + d) % GROUP
                home(j, to, me, to).start()

            @pl.when(me // GROUP == h)
            def _():
                pltpu.make_async_copy(got.at[j, me], back.at[j, me], br.at[j]).start()

            @pl.when(me // GROUP != h)
            def _():
                to = h * GROUP + me % GROUP
                home(j, to, me, to).start()

    def finish(j):
        pltpu.make_async_copy(got.at[j], back.at[j], br.at[j]).wait()
        flat = out_ref.reshape(CELLS * LEVELS, 128)
        light = glow[...]
        for p in range(PEERS):
            level = j * 8 + p
            top = back[j, p] + source_ref[pl.ds(level, 1), :] * light
            flat[pl.ds(level, CELLS, stride=LEVELS), :] = top / (
                1.0 + loss_ref[pl.ds(level, 1), :] * light
            )

    stages = ((filt, 2), (gather, 0), (onward, 2), (finish, 4), (spread, 3))

    def step(t, carry):
        for stage, lag in stages:

            @pl.when((t >= lag) & (t < lag + TILES))
            def _():
                stage(TILES - 1 - (t - lag))

        return carry

    lax.fori_loop(0, TILES + 4, step, 0)

    sent = pl.ds(0, PEERS - 1)
    pltpu.make_async_copy(dp.at[:, sent], dp.at[:, sent], fs).wait()
    pltpu.make_async_copy(got.at[:, sent], got.at[:, sent], bs).wait()
    edges, spectra = pl.ds(0, EDGE), pl.ds(EDGE, 2 * KPAD)
    pltpu.make_async_copy(given.at[:, edges], given.at[:, edges], es).wait()
    pltpu.make_async_copy(given.at[:, spectra], given.at[:, spectra], ss).wait()
    whole, part = rows.at[2], rows.at[2, :, half(0)]

    @pl.when(plain_north)
    def _():
        pltpu.make_async_copy(whole, whole, ls.at[0]).wait()

    @pl.when(plain_south)
    def _():
        pltpu.make_async_copy(whole, whole, ls.at[1]).wait()

    @pl.when(lat == 3)
    def _():
        pltpu.make_async_copy(part, part, ls.at[0]).wait()

    @pl.when(lat == 4)
    def _():
        pltpu.make_async_copy(part, part, ls.at[1]).wait()

    @pl.when(cross_row)
    def _():
        pltpu.make_async_copy(relay, relay, rs).wait()

    @pl.when(edge_row)
    def _():
        pltpu.make_async_copy(relay, relay, os).wait()


def body(tracers, offsets, fraction, cutoffs, keep_high, mixing, kz, light, loss_rate, source):
    project, rebuild, turn = wave_tables()
    levels, species = tracers.shape[2:]
    hbm = pl.BlockSpec(memory_space=pltpu.HBM)
    f32 = jnp.float32
    dma = pltpu.SemaphoreType.DMA
    operands = (
        offsets,
        fraction,
        cutoffs,
        keep_high,
        mixing,
        light,
        tracers.reshape(CELLS, levels, species),
        kz.reshape(CELLS, levels).T,
        jnp.asarray(turn),
        jnp.asarray(project),
        jnp.asarray(rebuild),
        loss_rate,
        source,
    )
    out = pl.pallas_call(
        kernel,
        out_shape=pltpu.VMEM((CELLS, levels, species), f32),
        in_specs=[hbm] * 13,
        out_specs=pl.BlockSpec(memory_space=pltpu.VMEM),
        scratch_shapes=[
            pltpu.SMEM((1,), jnp.int32),
            pltpu.SMEM((1,), f32),
            pltpu.SMEM((1,), jnp.int32),
            pltpu.SMEM((1,), f32),
            pltpu.SMEM((1,), f32),
            pltpu.SMEM((1, CELLS), f32),
            pltpu.VMEM((levels, CELLS), f32),
            pltpu.VMEM(turn.shape, f32),
            pltpu.VMEM(project.shape, jnp.bfloat16),
            pltpu.VMEM(rebuild.shape, jnp.bfloat16),
            pltpu.VMEM((levels, species), f32),
            pltpu.VMEM((levels, species), f32),
            pltpu.VMEM((TILES, CELLS, 8, 128), f32),
            pltpu.VMEM((CELLS, 128), f32),
            pltpu.VMEM((CELLS, 128), f32),
            pltpu.VMEM((128, 128), f32),
            pltpu.VMEM((TILES, PEERS, CELLS, 128), f32),
            pltpu.VMEM((TILES, PEERS, CELLS, 128), f32),
            pltpu.VMEM((TILES, PEERS, CELLS, 128), f32),
            pltpu.VMEM((TILES, HALF + 2 * EDGE, 128), f32),
            pltpu.VMEM((TILES, EDGE + 2 * KPAD, 128), f32),
            pltpu.VMEM((TILES, EDGE + 2 * KPAD, 128), f32),
            pltpu.VMEM((3, TILES, HALF, 128), f32),
            pltpu.VMEM((TILES, DIRECT, 128), f32),
            pltpu.VMEM((TILES, PEERS, CELLS, 128), f32),
            dma((TILES,)),
            dma,
            dma((TILES,)),
            dma,
            dma,
            dma((TILES,)),
            dma((2,)),
            dma((2, 2, TILES)),
            dma,
            dma((TILES,)),
            dma,
            dma,
            dma((TILES,)),
            dma((12,)),
        ],
        compiler_params=pltpu.CompilerParams(
            collective_id=0, has_side_effects=True, vmem_limit_bytes=46 << 20
        ),
        name="transport",
    )(*[pltpu.with_memory_space_constraint(x, pltpu.HBM) if x.size > 1 else x for x in operands])
    return out.reshape(tracers.shape)


def solution(mesh):
    return jax.shard_map(
        body,
        mesh=mesh,
        in_specs=(
            P("lat", "lon", None, None),
            P("lat"),
            P("lat"),
            P("lat"),
            P("lat"),
            P("lat"),
            P("lat", "lon", None),
            P("lat", "lon"),
            P(),
            P(),
        ),
        out_specs=P("lat", "lon", None, None),
        check_vma=False,
    )
```

time: 118 us -> 107 us (0.907)
  the two profiles are of different devices: /device:TPU:25 before, /device:TPU:87 now
where the time goes in v3:
time: 107 us
  Pallas kernels  102 us (95%)
  between operations  3.24 us (3%)
  local copies, waits for them, and re-layouts  1.72 us (2%)
    pallas_call x1, Pallas kernels, body(): pl.pallas_call(kernel, out_shape=pltpu.VMEM((CELLS, levels, species), f32...  102 us

profile of v3, /device:TPU:87, one launch (start us, length us, event | category | flops | bytes accessed | tf_op | source)
XLA Modules:
  0.0 107.3 jit_solution(11830248680818960027)
XLA Ops:
  3.2 102.3 %transport.1 = f32[90,72,128]{2,1,0:T(8,128)S(1)} custom-call(s32[1]{0:T(128)S(6)} %copy.16.off_hbm, f32[1]{0:T(128)S(6)} %copy.17.frac_hbm, s32[1]{0:T(128)S(6)} %copy.18.cut_hbm, f32[1]{0:T(128)S(6)} %copy.19.keep_hbm, f32[1]{0:T(128)S(6)} %copy.20.mix_hbm, f32[1,90]{1,0:T(1,128)} %light_hbm.1, f32[90,72,128]{2,1,0:T(8,128)} %bitcast.6, f32[72,90]{1,0:T(8,128)} %bitcast.7, ...), custom_call_target="tpu_custom_call" | custom-call | tf_op jit(solution)/shard_map/transport/pallas_call | solution.py:497
  105.5 1.7 %copy.15 = f32[1,90,72,128]{3,2,1,0:T(8,128)} copy(f32[1,90,72,128]{3,2,1,0:T(8,128)S(1)} %bitcast.5) | data formatting | bytes 6635520

commit v4 on v3

--- a/solution.py
+++ b/solution.py
@@ -22,6 +22,15 @@
 DIRECT = HALF // 2
 GROUP = PEERS // 2
 RELAYED = ((3, 7), (7, 3), (7, 4), (4, 7), (4, 0), (0, 4), (0, 3), (3, 0))
+LOW = 8
+FULL = ((0, 2 * KPAD),)
+CLASSES = (
+    (0, 0, 48, FULL),
+    (1, 2, 96, FULL),
+    (3, 4, 136, FULL),
+    (5, 6, EDGE, FULL),
+    (7, 7, EDGE, ((0, LOW), (KPAD, LOW))),
+)
 LEFT = EDGE
 RIGHT = EDGE + HALF
 
@@ -135,17 +144,21 @@
             got.at[j, src], back.at[j, dst], bs, br.at[j], device_id=peer(to), device_id_type=MESH
         )
 
-    def edge_copy(j):
+    def edge_copy(j, n):
         return pltpu.make_async_remote_copy(
-            given.at[j, pl.ds(0, EDGE)], taken.at[j, pl.ds(0, EDGE)], es, er.at[j],
+            given.at[j, pl.ds(EDGE - n, n)], taken.at[j, pl.ds(EDGE - n, n)], es, er.at[j],
             device_id=other, device_id_type=MESH,
         )
 
-    def spec_copy(j):
+    def spec_copy(j, first, count):
+        part = pl.ds(EDGE + first, count)
         return pltpu.make_async_remote_copy(
-            given.at[j, pl.ds(EDGE, 2 * KPAD)], taken.at[j, pl.ds(EDGE, 2 * KPAD)], ss, er.at[j],
+            given.at[j, part], taken.at[j, part], ss, er.at[j],
             device_id=other, device_id_type=MESH,
         )
+
+    def in_class(lo, hi):
+        return (lat >= lo) & (lat <= hi)
 
     def half(h):
         return pl.ds(h * DIRECT, DIRECT)
@@ -194,6 +207,11 @@
     for copy in arrivals[1:]:
         copy.start()
 
+    @pl.when(lat == 7)
+    def _():
+        for first, last in ((LOW, KPAD), (KPAD + LOW, 2 * KPAD)):
+            taken[:, EDGE + first : EDGE + last, :] = jnp.zeros((TILES, last - first, 128), jnp.float32)
+
     barrier = pltpu.get_barrier_semaphore()
     for d in range(1, PEERS):
         pl.semaphore_signal(barrier, inc=1, device_id=peer((me + d) % PEERS), device_id_type=MESH)
@@ -312,9 +330,14 @@
 
         for s in range(PEERS):
             circ[j, LEFT + CELLS * s : LEFT + CELLS * (s + 1), :] = got[j, s]
-        begin = jnp.clip(LEFT + (off + 1) * (HALF - EDGE), LEFT, RIGHT - EDGE)
-        given[j, 0:EDGE, :] = circ[j, pl.ds(begin, EDGE), :]
-        edge_copy(j).start()
+        for lo, hi, n, parts in CLASSES:
+
+            @pl.when(in_class(lo, hi))
+            def _():
+                begin = jnp.clip(LEFT + (off + 1) * HALF, LEFT, RIGHT - n)
+                given[j, EDGE - n : EDGE, :] = circ[j, pl.ds(begin, n), :]
+                edge_copy(j, n).start()
+
         field = circ[j, LEFT:RIGHT, :]
         high = field.astype(jnp.bfloat16)
         low = (field - high.astype(jnp.float32)).astype(jnp.bfloat16)
@@ -323,13 +346,24 @@
         )
         n = 2 * KPAD
         given[j, EDGE : EDGE + n, :] = part[:n, :128] + part[n:, :128] + part[:n, 128:]
-        spec_copy(j).start()
+        for lo, hi, n, parts in CLASSES:
+
+            @pl.when(in_class(lo, hi))
+            def _():
+                for first, count in parts:
+                    spec_copy(j, first, count).start()
 
     def filt(j):
-        pltpu.make_async_copy(given.at[j], taken.at[j], er.at[j]).wait()
-        fresh = taken[j, 0:EDGE, :]
-        circ[j, 0:EDGE, :] = fresh
-        circ[j, RIGHT : RIGHT + EDGE, :] = fresh
+        for lo, hi, n, parts in CLASSES:
+
+            @pl.when(in_class(lo, hi))
+            def _():
+                come = pl.ds(0, n + sum(count for _, count in parts))
+                pltpu.make_async_copy(given.at[j, come], taken.at[j, come], er.at[j]).wait()
+                fresh = taken[j, EDGE - n : EDGE, :]
+                circ[j, LEFT - n : LEFT, :] = fresh
+                circ[j, RIGHT : RIGHT + n, :] = fresh
+
         level = lax.broadcasted_iota(jnp.int32, (KPAD, 128), 0)
         sign = jnp.where(level % 2 == 0, 1.0, -1.0)
         cosine, sine = slice(EDGE, EDGE + KPAD), slice(EDGE + KPAD, EDGE + 2 * KPAD)
@@ -443,9 +477,15 @@
     sent = pl.ds(0, PEERS - 1)
     pltpu.make_async_copy(dp.at[:, sent], dp.at[:, sent], fs).wait()
     pltpu.make_async_copy(got.at[:, sent], got.at[:, sent], bs).wait()
-    edges, spectra = pl.ds(0, EDGE), pl.ds(EDGE, 2 * KPAD)
-    pltpu.make_async_copy(given.at[:, edges], given.at[:, edges], es).wait()
-    pltpu.make_async_copy(given.at[:, spectra], given.at[:, spectra], ss).wait()
+    for lo, hi, n, parts in CLASSES:
+
+        @pl.when(in_class(lo, hi))
+        def _():
+            edges = given.at[:, pl.ds(0, n)]
+            spectra = given.at[:, pl.ds(0, sum(count for _, count in parts))]
+            pltpu.make_async_copy(edges, edges, es).wait()
+            pltpu.make_async_copy(spectra, spectra, ss).wait()
+
     whole, part = rows.at[2], rows.at[2, :, half(0)]
 
     @pl.when(plain_north)

time: 107 us -> 106 us (level)
  no operation moved by 1% of the time
where the time goes in v4:
time: 106 us
  Pallas kernels  101 us (95%)
  between operations  3.24 us (3%)
  local copies, waits for them, and re-layouts  1.72 us (2%)
    pallas_call x1, Pallas kernels, body(): pl.pallas_call(kernel, out_shape=pltpu.VMEM((CELLS, levels, species), f32...  101 us

profile of v4, /device:TPU:87, one launch (start us, length us, event | category | flops | bytes accessed | tf_op | source)
XLA Modules:
  0.0 106.3 jit_solution(5454936424046764226)
XLA Ops:
  3.2 101.3 %transport.1 = f32[90,72,128]{2,1,0:T(8,128)S(1)} custom-call(s32[1]{0:T(128)S(6)} %copy.16.off_hbm, f32[1]{0:T(128)S(6)} %copy.17.frac_hbm, s32[1]{0:T(128)S(6)} %copy.18.cut_hbm, f32[1]{0:T(128)S(6)} %copy.19.keep_hbm, f32[1]{0:T(128)S(6)} %copy.20.mix_hbm, f32[1,90]{1,0:T(1,128)} %light_hbm.1, f32[90,72,128]{2,1,0:T(8,128)} %bitcast.6, f32[72,90]{1,0:T(8,128)} %bitcast.7, ...), custom_call_target="tpu_custom_call" | custom-call | tf_op jit(solution)/shard_map/transport/pallas_call | solution.py:537
  104.6 1.7 %copy.15 = f32[1,90,72,128]{3,2,1,0:T(8,128)} copy(f32[1,90,72,128]{3,2,1,0:T(8,128)S(1)} %bitcast.5) | data formatting | bytes 6635520

commit v5 on v4

--- a/solution.py
+++ b/solution.py
@@ -286,15 +286,23 @@
 
         @pl.when(c == 0)
         def _():
-            send(j)
+            send(j, 0)
 
         return x
 
-    def send(j):
-        for d in range(1, PEERS):
-            to = (me + d) % PEERS
+    def send(j, core):
+        for d in range(1, GROUP):
+            to = (me // 2 + d) % GROUP * 2 + core
             forth(j, to, me, to).start()
-        pltpu.make_async_copy(dp.at[j, me], got.at[j, me], fr.at[j]).start()
+        near = me // 2 * 2 + core
+
+        @pl.when(near == me)
+        def _():
+            pltpu.make_async_copy(dp.at[j, me], got.at[j, me], fr.at[j]).start()
+
+        @pl.when(near != me)
+        def _():
+            forth(j, near, me, near).start()
 
     lax.fori_loop(0, TILES, up, zero)
 
@@ -317,16 +325,20 @@
     turn = (1.0 - frac) * turn_ref[pl.ds(EDGE + off, 1), :] + frac * turn_ref[pl.ds(EDGE + 1 + off, 1), :]
     rot[...] = jnp.broadcast_to(turn * share, (128, 128)).T
 
+    send(TILES - 1, 1)
+
     def gather(j):
         pltpu.make_async_copy(dp.at[j], got.at[j], fr.at[j]).wait()
 
         @pl.when(j == TILES - 1)
         def _():
-            send(j - 1)
+            send(j - 1, 0)
+            send(j - 1, 1)
 
         @pl.when(j >= 2)
         def _():
-            send(j - 2)
+            send(j - 2, 0)
+            send(j - 2, 1)
 
         for s in range(PEERS):
             circ[j, LEFT + CELLS * s : LEFT + CELLS * (s + 1), :] = got[j, s]

time: 106 us -> 106 us (level)
  no operation moved by 1% of the time
where the time goes in v5:
time: 106 us
  Pallas kernels  101 us (95%)
  between operations  3.24 us (3%)
  local copies, waits for them, and re-layouts  1.72 us (2%)
    pallas_call x1, Pallas kernels, body(): pl.pallas_call(kernel, out_shape=pltpu.VMEM((CELLS, levels, species), f32...  101 us

profile of v5, /device:TPU:87, one launch (start us, length us, event | category | flops | bytes accessed | tf_op | source)
XLA Modules:
  0.0 105.6 jit_solution(10150859981935769299)
XLA Ops:
  3.2 100.7 %transport.1 = f32[90,72,128]{2,1,0:T(8,128)S(1)} custom-call(s32[1]{0:T(128)S(6)} %copy.16.off_hbm, f32[1]{0:T(128)S(6)} %copy.17.frac_hbm, s32[1]{0:T(128)S(6)} %copy.18.cut_hbm, f32[1]{0:T(128)S(6)} %copy.19.keep_hbm, f32[1]{0:T(128)S(6)} %copy.20.mix_hbm, f32[1,90]{1,0:T(1,128)} %light_hbm.1, f32[90,72,128]{2,1,0:T(8,128)} %bitcast.6, f32[72,90]{1,0:T(8,128)} %bitcast.7, ...), custom_call_target="tpu_custom_call" | custom-call | tf_op jit(solution)/shard_map/transport/pallas_call | solution.py:549
  103.9 1.7 %copy.15 = f32[1,90,72,128]{3,2,1,0:T(8,128)} copy(f32[1,90,72,128]{3,2,1,0:T(8,128)S(1)} %bitcast.5) | data formatting | bytes 6635520

commit v6 on v5

--- a/solution.py
+++ b/solution.py
@@ -473,18 +473,22 @@
                 1.0 + loss_ref[pl.ds(level, 1), :] * light
             )
 
-    stages = ((filt, 2), (gather, 0), (onward, 2), (finish, 4), (spread, 3))
+    stages = ((filt, 2), (gather, 0), (onward, 2), (spread, 3), (finish, 5))
 
     def step(t, carry):
+        @pl.when(t == 1)
+        def _():
+            filt(TILES - 1)
+
         for stage, lag in stages:
 
-            @pl.when((t >= lag) & (t < lag + TILES))
+            @pl.when((t >= lag + (stage is filt)) & (t < lag + TILES))
             def _():
                 stage(TILES - 1 - (t - lag))
 
         return carry
 
-    lax.fori_loop(0, TILES + 4, step, 0)
+    lax.fori_loop(0, TILES + 5, step, 0)
 
     sent = pl.ds(0, PEERS - 1)
     pltpu.make_async_copy(dp.at[:, sent], dp.at[:, sent], fs).wait()

time: 106 us -> 102 us (0.962); the launches traced: 106 us -> 100 us
  Pallas kernels: 101 us -> 95.5 us
    pallas_call x1, Pallas kernels: 101 us -> 95.5 us  [body(): pl.pallas_call(kernel, out_shape=pltpu.VMEM((CELLS, levels, species), f32...]
where the time goes in v6:
time: 102 us; the launch traced here: 100 us
  Pallas kernels  95.5 us (94%)
  between operations  3.24 us (3%)
  local copies, waits for them, and re-layouts  1.72 us (2%)
    pallas_call x1, Pallas kernels, body(): pl.pallas_call(kernel, out_shape=pltpu.VMEM((CELLS, levels, species), f32...  95.5 us

profile of v6, /device:TPU:87, one launch (start us, length us, event | category | flops | bytes accessed | tf_op | source)
XLA Modules:
  0.0 100.5 jit_solution(15319553970344230523)
XLA Ops:
  3.2 95.5 %transport.1 = f32[90,72,128]{2,1,0:T(8,128)S(1)} custom-call(s32[1]{0:T(128)S(6)} %copy.16.off_hbm, f32[1]{0:T(128)S(6)} %copy.17.frac_hbm, s32[1]{0:T(128)S(6)} %copy.18.cut_hbm, f32[1]{0:T(128)S(6)} %copy.19.keep_hbm, f32[1]{0:T(128)S(6)} %copy.20.mix_hbm, f32[1,90]{1,0:T(1,128)} %light_hbm.1, f32[90,72,128]{2,1,0:T(8,128)} %bitcast.6, f32[72,90]{1,0:T(8,128)} %bitcast.7, ...), custom_call_target="tpu_custom_call" | custom-call | tf_op jit(solution)/shard_map/transport/pallas_call | solution.py:553
  98.8 1.7 %copy.15 = f32[1,90,72,128]{3,2,1,0:T(8,128)} copy(f32[1,90,72,128]{3,2,1,0:T(8,128)S(1)} %bitcast.5) | data formatting | bytes 6635520

commit v7 on v6

--- a/solution.py
+++ b/solution.py
@@ -473,7 +473,7 @@
                 1.0 + loss_ref[pl.ds(level, 1), :] * light
             )
 
-    stages = ((filt, 2), (gather, 0), (onward, 2), (spread, 3), (finish, 5))
+    stages = ((filt, 2), (gather, 0), (spread, 3), (onward, 2), (finish, 5))
 
     def step(t, carry):
         @pl.when(t == 1)

time: 102 us -> 102 us (level)
  no operation moved by 1% of the time
where the time goes in v7:
time: 102 us; the launch traced here: 100 us
  Pallas kernels  95.5 us (94%)
  between operations  3.24 us (3%)
  local copies, waits for them, and re-layouts  1.72 us (2%)
    pallas_call x1, Pallas kernels, body(): pl.pallas_call(kernel, out_shape=pltpu.VMEM((CELLS, levels, species), f32...  95.5 us

profile of v7, /device:TPU:87, one launch (start us, length us, event | category | flops | bytes accessed | tf_op | source)
XLA Modules:
  0.0 100.5 jit_solution(2621234226055853871)
XLA Ops:
  3.2 95.5 %transport.1 = f32[90,72,128]{2,1,0:T(8,128)S(1)} custom-call(s32[1]{0:T(128)S(6)} %copy.16.off_hbm, f32[1]{0:T(128)S(6)} %copy.17.frac_hbm, s32[1]{0:T(128)S(6)} %copy.18.cut_hbm, f32[1]{0:T(128)S(6)} %copy.19.keep_hbm, f32[1]{0:T(128)S(6)} %copy.20.mix_hbm, f32[1,90]{1,0:T(1,128)} %light_hbm.1, f32[90,72,128]{2,1,0:T(8,128)} %bitcast.6, f32[72,90]{1,0:T(8,128)} %bitcast.7, ...), custom_call_target="tpu_custom_call" | custom-call | tf_op jit(solution)/shard_map/transport/pallas_call | solution.py:553
  98.8 1.7 %copy.15 = f32[1,90,72,128]{3,2,1,0:T(8,128)} copy(f32[1,90,72,128]{3,2,1,0:T(8,128)S(1)} %bitcast.5) | data formatting | bytes 6635520

commit v8 on v7

--- a/solution.py
+++ b/solution.py
@@ -305,6 +305,7 @@
             forth(j, near, me, near).start()
 
     lax.fori_loop(0, TILES, up, zero)
+    send(TILES - 1, 1)
 
     for copy in arrivals[1:]:
         copy.wait()
@@ -324,8 +325,6 @@
     share = jnp.where(wave <= cut_ref[0], jnp.where(wave == 0, 1.0, 2.0) / NLON, 0.0) * (1.0 - keep)
     turn = (1.0 - frac) * turn_ref[pl.ds(EDGE + off, 1), :] + frac * turn_ref[pl.ds(EDGE + 1 + off, 1), :]
     rot[...] = jnp.broadcast_to(turn * share, (128, 128)).T
-
-    send(TILES - 1, 1)
 
     def gather(j):
         pltpu.make_async_copy(dp.at[j], got.at[j], fr.at[j]).wait()

time: 102 us -> 102 us (level)
  no operation moved by 1% of the time
where the time goes in v8:
time: 102 us; the launch traced here: 100 us
  Pallas kernels  95.5 us (94%)
  between operations  3.24 us (3%)
  local copies, waits for them, and re-layouts  1.72 us (2%)
    pallas_call x1, Pallas kernels, body(): pl.pallas_call(kernel, out_shape=pltpu.VMEM((CELLS, levels, species), f32...  95.5 us

profile of v8, /device:TPU:87, one launch (start us, length us, event | category | flops | bytes accessed | tf_op | source)
XLA Modules:
  0.0 100.4 jit_solution(4373536111311331785)
XLA Ops:
  3.2 95.5 %transport.1 = f32[90,72,128]{2,1,0:T(8,128)S(1)} custom-call(s32[1]{0:T(128)S(6)} %copy.16.off_hbm, f32[1]{0:T(128)S(6)} %copy.17.frac_hbm, s32[1]{0:T(128)S(6)} %copy.18.cut_hbm, f32[1]{0:T(128)S(6)} %copy.19.keep_hbm, f32[1]{0:T(128)S(6)} %copy.20.mix_hbm, f32[1,90]{1,0:T(1,128)} %light_hbm.1, f32[90,72,128]{2,1,0:T(8,128)} %bitcast.6, f32[72,90]{1,0:T(8,128)} %bitcast.7, ...), custom_call_target="tpu_custom_call" | custom-call | tf_op jit(solution)/shard_map/transport/pallas_call | solution.py:552
  98.7 1.7 %copy.15 = f32[1,90,72,128]{3,2,1,0:T(8,128)} copy(f32[1,90,72,128]{3,2,1,0:T(8,128)S(1)} %bitcast.5) | data formatting | bytes 6635520

commit v9 on v7

--- a/solution.py
+++ b/solution.py
@@ -28,7 +28,8 @@
     (0, 0, 48, FULL),
     (1, 2, 96, FULL),
     (3, 4, 136, FULL),
-    (5, 6, EDGE, FULL),
+    (5, 5, 160, FULL),
+    (6, 6, EDGE, FULL),
     (7, 7, EDGE, ((0, LOW), (KPAD, LOW))),
 )
 LEFT = EDGE

time: 102 us -> 102 us (level)
  no operation moved by 1% of the time
where the time goes in v9:
time: 102 us; the launch traced here: 100 us
  Pallas kernels  95.5 us (94%)
  between operations  3.24 us (3%)
  local copies, waits for them, and re-layouts  1.72 us (2%)
    pallas_call x1, Pallas kernels, body(): pl.pallas_call(kernel, out_shape=pltpu.VMEM((CELLS, levels, species), f32...  95.5 us

profile of v9, /device:TPU:87, one launch (start us, length us, event | category | flops | bytes accessed | tf_op | source)
XLA Modules:
  0.0 100.5 jit_solution(939969623289118123)
XLA Ops:
  3.2 95.5 %transport.1 = f32[90,72,128]{2,1,0:T(8,128)S(1)} custom-call(s32[1]{0:T(128)S(6)} %copy.16.off_hbm, f32[1]{0:T(128)S(6)} %copy.17.frac_hbm, s32[1]{0:T(128)S(6)} %copy.18.cut_hbm, f32[1]{0:T(128)S(6)} %copy.19.keep_hbm, f32[1]{0:T(128)S(6)} %copy.20.mix_hbm, f32[1,90]{1,0:T(1,128)} %light_hbm.1, f32[90,72,128]{2,1,0:T(8,128)} %bitcast.6, f32[72,90]{1,0:T(8,128)} %bitcast.7, ...), custom_call_target="tpu_custom_call" | custom-call | tf_op jit(solution)/shard_map/transport/pallas_call | solution.py:554
  98.8 1.7 %copy.15 = f32[1,90,72,128]{3,2,1,0:T(8,128)} copy(f32[1,90,72,128]{3,2,1,0:T(8,128)S(1)} %bitcast.5) | data formatting | bytes 6635520
